TPU v7x, 256 devices: a whole 4x4x8 slice. The times are simulated.
256 devices in a mesh: rows: 64 (over z, y, core), cols: 4 (over x).
Axes of the slice: x: 4, y: 4, z: 8, core: 2. Of those that a mesh axis runs over, the one named last changes fastest.
Arguments:
- points: float32 [65536, 1024], P('rows', 'cols'), may hold values from -6 to 6
- pivots: int32 [2, 512], replicated, may hold values from 0 to 65535, as said below
- targets: float32 [65536, 256], P('rows', 'cols'), may hold values from -6 to 6
Outputs:
- factor: float32 [65536, 1024], P(('rows', 'cols'))
- projection: float32 [1024, 256], P(None, 'cols')
Inputs may be any that keep to these rules, and one draw needn't show every extreme that they name: All 1024 indices of both blocks are distinct. The points of one index of rows (an aligned run of 1024 indices) hold at most 64 pivots of the two blocks together, and in every draw some index of rows holds exactly 64.
All inputs are finite; a program needn't handle non-finite values.
Results may differ from a plain program's by a relative error of at most 0.0003.
Values sent between devices are 32-bit elements; how exact they have to be, the bound alone decides.
A program may use at most 64 MiB of HBM per device.

v0:
```python
import math
import jax
import jax.numpy as jnp
from jax import lax
from jax.sharding import Mesh
from jax.sharding import PartitionSpec as P

E = 1024
ROWS = ("rows_0", "rows_1", "rows_2")
ROWS_COLS = ("rows_0", "rows_1", "rows_2", "cols")
RIDGE = 0.001


def in_blocks(value, dim, count):
    before, after = (value.shape[:dim], value.shape[dim + 1 :])
    return jnp.moveaxis(value.reshape(*before, count, -1, *after), dim, 0)


def summed_on_arrival(value, axis, dim):
    count = lax.axis_size(axis)
    blocks = lax.all_to_all(in_blocks(value, dim, count), axis, 0, 0, tiled=True)
    return jnp.sum(blocks, axis=0)


def sum_by_axis(value, axes, dim):
    far, near = axes
    blocks = in_blocks(value, dim, lax.axis_size(far))
    nearer = summed_on_arrival(blocks, near, dim + 1)
    arrived = lax.all_to_all(nearer, far, split_axis=0, concat_axis=0, tiled=True)
    return arrived.sum(axis=0)


def padded_to(lines, count):
    spare = -lines.shape[0] % count
    if not spare:
        return lines
    return jnp.concatenate([lines, jnp.zeros((spare, *lines.shape[1:]), lines.dtype)])


def copy_for_each(value, axis):
    copies = jnp.broadcast_to(value, (lax.axis_size(axis), *value.shape))
    return lax.all_to_all(copies, axis, split_axis=0, concat_axis=0, tiled=True)


def in_order(blocks, dim):
    blocks = jnp.moveaxis(blocks, 0, dim)
    lengths = blocks.shape
    return blocks.reshape(*lengths[:dim], lengths[dim] * lengths[dim + 1], *lengths[dim + 2 :])


def gather_axes(value, axes, dim):
    far, near = axes
    leading = copy_for_each(value, far)
    blocks = jnp.swapaxes(copy_for_each(leading, near), 0, 1)
    return in_order(blocks.reshape(-1, *value.shape), dim)


def sum_by_parts(value, axes):
    lines = value.reshape(-1, value.shape[-1])
    own = sum_by_axis(padded_to(lines, lax.axis_size(axes[0]) * lax.axis_size(axes[1])), axes, 0)
    whole = gather_axes(own, axes, 0)
    return whole[: len(lines)].reshape(value.shape)


def right_side_solve(low, values):
    return lax.linalg.triangular_solve(low, values, left_side=False, lower=True, transpose_a=True)


def shards(points, pivots, targets):
    highest = lax.Precision.HIGHEST
    rows_dev = points.shape[0]
    nrows = lax.axis_size(ROWS)
    row_me = lax.axis_index(ROWS)
    block = pivots.shape[1]
    flat = pivots.reshape(-1)
    owner = flat // rows_dev
    inside = flat - owner * rows_dev
    mine = owner == row_me
    picked = jnp.where(mine[:, None], points[inside], 0.0)
    pivot_part = sum_by_parts(picked, (("rows_0", "rows_1"), "rows_2"))
    own_rows = lax.all_to_all(points, "cols", split_axis=0, concat_axis=1, tiled=True)
    pivot_full = lax.all_gather(pivot_part, "cols", axis=1, tiled=True)
    own_norms = jnp.sum(own_rows * own_rows, axis=1)
    full_norms = jnp.sum(pivot_full * pivot_full, axis=1)
    cross = jnp.dot(own_rows, pivot_full.T, precision=highest, preferred_element_type=jnp.float32)
    dist = own_norms[:, None] + full_norms[None, :] - 2.0 * cross
    kern = jnp.exp(-dist / (2.0 * E))
    first = kern[:, :block]
    second = kern[:, block:]
    identity = jnp.eye(block, dtype=jnp.float32)
    every_norms = jnp.sum(pivot_full * pivot_full, axis=1)
    pivot_cross = jnp.dot(
        pivot_full, pivot_full.T, precision=highest, preferred_element_type=jnp.float32
    )
    pivot_kern = jnp.exp(
        -(every_norms[:, None] + every_norms[None, :] - 2.0 * pivot_cross) / (2.0 * E)
    )
    low_one = jnp.linalg.cholesky(pivot_kern[:block, :block] + RIDGE * identity)
    factor_one = right_side_solve(low_one, first)
    crossed = right_side_solve(low_one, pivot_kern[block:, :block])
    second_pivot = pivot_kern[block:, block:]
    resid = second - jnp.dot(
        factor_one, crossed.T, precision=highest, preferred_element_type=jnp.float32
    )
    schur = second_pivot - jnp.dot(
        crossed, crossed.T, precision=highest, preferred_element_type=jnp.float32
    )
    low_two = jnp.linalg.cholesky(schur + RIDGE * identity)
    second_lower_matrix = right_side_solve(low_two, resid)
    factor = jnp.concatenate([factor_one, second_lower_matrix], axis=1)
    scaling = 1.0 / math.sqrt(rows_dev * nrows)
    summed = lax.dot_general(
        lax.all_gather(factor, "cols", axis=0, tiled=True),
        targets,
        (((0,), (0,)), ((), ())),
        precision=highest,
        preferred_element_type=jnp.float32,
    )
    projection = sum_by_parts(summed, (("rows_0", "rows_1"), "rows_2")) * scaling
    return (factor, projection)


def solution(mesh):
    finer = Mesh(
        mesh.devices.reshape(8, 4, 2, mesh.shape["cols"]), ("rows_0", "rows_1", "rows_2", "cols")
    )
    placed = (P(ROWS, "cols"), P(), P(ROWS, "cols"))
    return jax.shard_map(
        shards,
        mesh=finer,
        in_specs=placed,
        out_specs=(P(ROWS_COLS, None), P(None, "cols")),
        check_vma=False,
    )
```

profile of v0, /device:TPU:1, one launch (start us, length us, event | category | flops | bytes accessed | tf_op | source)
XLA Modules:
  0.0 562.3 jit_solution(10327082064744761221)
XLA Ops:
  9.0 4.7 gather_fusion
  14.8 6.8 %all-to-all-start = ((f32[2,32,16,256]{3,2,1,0:T(8,128)}), f32[2,32,16,256]{3,2,1,0:T(8,128)S(1)}, u32[]{:S(2)}, u32[]{:S(2)}) async-start(f32[2,32,16,256]{3,2,1,0:T(8,128)} %fusion.7), calls=%async_computation | async-start | bytes 2097152 | tf_op jit(solution)/shard_map/all_to_all | solution.py:21
  23.5 25.9 %all_to_all.63 = f32[32,16,256]{2,1,0:T(8,128)S(1)} all-to-all(f32[32,16,256]{2,1,0:T(8,128)S(1)} %reduce_sum.58), channel_id=1, replica_groups=mesh['rows_0'=8,'rows_1'=4,'rows_2'=2,'cols'=4] {'rows_0','rows_1'}, dimensions={0} | all-to-all | bytes 1048576 | tf_op jit(solution)/shard_map/all_to_all | solution.py:29
  49.5 20.1 %all_to_all.59 = f32[32,16,256]{2,1,0:T(8,128)S(1)} all-to-all(f32[32,16,256]{2,1,0:T(8,128)S(1)} %broadcast_in_dim.33), channel_id=1, replica_groups=mesh['rows_0'=8,'rows_1'=4,'rows_2'=2,'cols'=4] {'rows_0','rows_1'}, dimensions={0} | all-to-all | bytes 1048576 | tf_op jit(solution)/shard_map/all_to_all | solution.py:42
  69.7 7.8 %all_to_all.60 = f32[2,32,16,256]{3,2,1,0:T(8,128)S(1)} all-to-all(f32[2,32,16,256]{3,2,1,0:T(8,128)S(1)} %broadcast_in_dim.34), channel_id=1, replica_groups=mesh['rows_0'=8,'rows_1'=4,'rows_2'=2,'cols'=4] {'rows_2'}, dimensions={0} | all-to-all | bytes 2097152 | tf_op jit(solution)/shard_map/all_to_all | solution.py:42
  83.2 19.1 %all-to-all-done.4 = f32[4,256,256]{2,1,0:T(8,128)S(1)} async-done(((f32[4,256,256]{2,1,0:T(8,128)}), f32[4,256,256]{2,1,0:T(8,128)S(1)}, u32[]{:S(2)}, u32[]{:S(2)}) %all-to-all-start.4) | async-done | bytes 1048608 | tf_op jit(solution)/shard_map/all_to_all | solution.py:81
  102.8 29.1 %all-gather.3.cloned.1.call-done = f32[1024,1024]{1,0:T(8,128)} async-done(((f32[1024,256]{1,0:T(8,128)}), f32[1024,1024]{1,0:T(8,128)}) %all-gather.3.cloned.1.call-update) | async-done | bytes 4194320 | tf_op jit(solution)/shard_map/all_gather | solution.py:82
  135.4 14.4 %multiply_exponential_fusion = f32[1024,1024]{0,1:T(8,128)S(1)} fusion(f32[1024,1024]{1,0:T(8,128)S(1)} %copy-done.1, f32[1024]{0:T(1024)S(1)} %multiply_reduce_fusion), kind=kOutput, calls=%fused_computation.5 | convolution fusion | flops 12890144768 | bytes 8392704 | tf_op jit(solution)/shard_map/dot_general | solution.py:92
  153.7 11.7 %cholesky.286 = f32[128,128]{1,0:T(8,128)S(1)} custom-call(f32[128,128]{1,0:T(8,128)S(1)} %cholesky.426), custom_call_target="Cholesky" | custom-call | tf_op jit(solution)/shard_map/jit(cholesky)/cholesky | solution.py:98
  165.5 9.8 %custom-call.31 = f32[1,128,128]{1,2,0:T(8,128)S(1)} custom-call(f32[1,128,128]{2,1,0:T(8,128)S(1)} %get-tuple-element.123), custom_call_target="InvertDiagBlocksLowerTriangular" | custom-call | tf_op jit(solution)/shard_map/jit(cholesky)/cholesky | solution.py:98
  176.8 12.1 %cholesky.305 = f32[128,128]{1,0:T(8,128)S(1)} custom-call(f32[128,128]{1,0:T(8,128)S(1)} %cholesky.430), custom_call_target="Cholesky" | custom-call | tf_op jit(solution)/shard_map/jit(cholesky)/cholesky | solution.py:98
  189.1 10.4 %custom-call.32 = f32[1,128,128]{1,2,0:T(8,128)} custom-call(f32[1,128,128]{2,1,0:T(8,128)S(1)} %get-tuple-element.121), custom_call_target="InvertDiagBlocksLowerTriangular" | custom-call | tf_op jit(solution)/shard_map/jit(cholesky)/cholesky | solution.py:98
  203.3 11.7 %cholesky.326 = f32[128,128]{1,0:T(8,128)S(1)} custom-call(f32[128,128]{1,0:T(8,128)S(1)} %cholesky.435), custom_call_target="Cholesky" | custom-call | tf_op jit(solution)/shard_map/jit(cholesky)/cholesky | solution.py:98
  215.2 9.8 %custom-call.33 = f32[1,128,128]{1,2,0:T(8,128)S(1)} custom-call(f32[1,128,128]{2,1,0:T(8,128)S(1)} %get-tuple-element.119), custom_call_target="InvertDiagBlocksLowerTriangular" | custom-call | tf_op jit(solution)/shard_map/jit(cholesky)/cholesky | solution.py:98
  226.6 11.9 %cholesky.343 = f32[128,128]{1,0:T(8,128)S(1)} custom-call(f32[128,128]{1,0:T(8,128)S(1)} %convolution_subtract_fusion.16), custom_call_target="Cholesky" | custom-call | tf_op jit(solution)/shard_map/jit(cholesky)/cholesky | solution.py:98
  243.8 8.5 %while.5 = (s32[]{:T(128)}, f32[512,512]{0,1:T(8,128)S(1)}, s32[4,2]{0,1:T(2,128)S(1)}, f32[4,128,128]{2,1,0:T(8,128)S(1)}, s32[]{:T(128)}) while((s32[]{:T(128)}, f32[512,512]{0,1:T(8,128)S(1)}, s32[4,2]{0,1:T(2,128)S(1)}, f32[4,128,128]{2,1,0:T(8,128)S(1)}, s32[]{:T(128)}) %tuple.72), condition=%wide.while_cond, body=%wide.while_body.sunk | while | flops 2 | bytes 393329 | solution.py:66
  252.3 39.3 %custom-call.34 = f32[4,128,128]{1,2,0:T(8,128)S(1)} custom-call(f32[4,128,128]{2,1,0:T(8,128)S(1)} %get-tuple-element.26), custom_call_target="InvertDiagBlocksLowerTriangular" | custom-call | tf_op jit(solution)/shard_map/triangular_solve/custom-call.3 | solution.py:66
  293.0 5.5 fusion.4
  313.3 12.1 %cholesky.358 = f32[128,128]{1,0:T(8,128)S(1)} custom-call(f32[128,128]{1,0:T(8,128)S(1)} %cholesky.439), custom_call_target="Cholesky" | custom-call | tf_op jit(solution)/shard_map/jit(cholesky)/cholesky | solution.py:108
  326.1 9.8 %custom-call.35 = f32[1,128,128]{1,2,0:T(8,128)S(1)} custom-call(f32[1,128,128]{2,1,0:T(8,128)S(1)} %get-tuple-element.117), custom_call_target="InvertDiagBlocksLowerTriangular" | custom-call | tf_op jit(solution)/shard_map/jit(cholesky)/cholesky | solution.py:108
  336.7 11.7 %cholesky.377 = f32[128,128]{1,0:T(8,128)S(1)} custom-call(f32[128,128]{1,0:T(8,128)S(1)} %cholesky.443), custom_call_target="Cholesky" | custom-call | tf_op jit(solution)/shard_map/jit(cholesky)/cholesky | solution.py:108
  349.1 9.8 %custom-call.36 = f32[1,128,128]{1,2,0:T(8,128)S(1)} custom-call(f32[1,128,128]{2,1,0:T(8,128)S(1)} %get-tuple-element.114), custom_call_target="InvertDiagBlocksLowerTriangular" | custom-call | tf_op jit(solution)/shard_map/jit(cholesky)/cholesky | solution.py:108
  359.6 11.9 %cholesky.398 = f32[128,128]{1,0:T(8,128)S(1)} custom-call(f32[128,128]{1,0:T(8,128)S(1)} %cholesky.448), custom_call_target="Cholesky" | custom-call | tf_op jit(solution)/shard_map/jit(cholesky)/cholesky | solution.py:108
  372.1 9.8 %custom-call.37 = f32[1,128,128]{1,2,0:T(8,128)S(1)} custom-call(f32[1,128,128]{2,1,0:T(8,128)S(1)} %get-tuple-element.111), custom_call_target="InvertDiagBlocksLowerTriangular" | custom-call | tf_op jit(solution)/shard_map/jit(cholesky)/cholesky | solution.py:108
  382.6 11.7 %cholesky.415 = f32[128,128]{1,0:T(8,128)S(1)} custom-call(f32[128,128]{1,0:T(8,128)S(1)} %convolution_subtract_fusion.15), custom_call_target="Cholesky" | custom-call | tf_op jit(solution)/shard_map/jit(cholesky)/cholesky | solution.py:108
  397.7 8.1 %while.6 = (s32[]{:T(128)}, f32[512,512]{1,0:T(8,128)S(1)}, s32[4,2]{0,1:T(2,128)S(1)}, f32[4,128,128]{2,1,0:T(8,128)S(1)}, s32[]{:T(128)}) while((s32[]{:T(128)}, f32[512,512]{1,0:T(8,128)S(1)}, s32[4,2]{0,1:T(2,128)S(1)}, f32[4,128,128]{2,1,0:T(8,128)S(1)}, s32[]{:T(128)}) %tuple.82), condition=%wide.while_cond.clone, body=%wide.while_body.clone.sunk | while | flops 2 | bytes 131189 | solution.py:66
  405.8 39.5 %custom-call.38 = f32[4,128,128]{1,2,0:T(8,128)S(1)} custom-call(f32[4,128,128]{2,1,0:T(8,128)S(1)} %get-tuple-element.27), custom_call_target="InvertDiagBlocksLowerTriangular" | custom-call | tf_op jit(solution)/shard_map/triangular_solve/custom-call.3 | solution.py:66
  452.3 45.2 %all-gather.5.cloned.1.call-done = f32[1024,1024]{0,1:T(8,128)} async-done(((f32[256,1024]{0,1:T(8,128)}), f32[1024,1024]{0,1:T(8,128)}) %all-gather.5.cloned.1.call-update) | async-done | bytes 4194320 | tf_op jit(solution)/shard_map/all_gather | solution.py:113
  497.5 5.2 fusion.98
  510.0 18.7 %all_to_all.64 = f32[32,1,1024]{2,1,0:T(1,128)S(1)} all-to-all(f32[32,1,1024]{2,1,0:T(1,128)S(1)} %reshape.232), channel_id=1, replica_groups=mesh['rows_0'=8,'rows_1'=4,'rows_2'=2,'cols'=4] {'rows_0','rows_1'}, dimensions={0} | all-to-all | bytes 262144 | tf_op jit(solution)/shard_map/all_to_all | solution.py:29
  536.0 8.0 %all-to-all-done.7 = f32[32,1,1024]{2,1,0:T(1,128)S(1)} async-done(((f32[32,1,1024]{2,1,0:T(1,128)}), f32[32,1,1024]{2,1,0:T(1,128)S(1)}, u32[]{:S(2)}, u32[]{:S(2)}) %all-to-all-start.7) | async-done | bytes 131104 | tf_op jit(solution)/shard_map/all_to_all | solution.py:42
  545.5 6.9 %all_to_all.62 = f32[2,1,32768]{2,1,0:T(1,128)S(1)} all-to-all(f32[2,1,32768]{2,1,0:T(1,128)S(1)} %reshape.236), channel_id=1, replica_groups=mesh['rows_0'=8,'rows_1'=4,'rows_2'=2,'cols'=4] {'rows_2'}, dimensions={0} | all-to-all | bytes 524288 | tf_op jit(solution)/shard_map/all_to_all | solution.py:42
  (181 shorter events, 91.6 us)
Async XLA Ops:
  7.2 490.3 %copy-start = (f32[1024,64]{0,1:T(8,128)S(1)}, f32[1024,64]{0,1:T(8,128)}, u32[]{:S(2)}) copy-start(f32[1024,64]{0,1:T(8,128)} %param.8) | copy-start | bytes 786436
  14.8 8.6 %all-to-all-start = ((f32[2,32,16,256]{3,2,1,0:T(8,128)}), f32[2,32,16,256]{3,2,1,0:T(8,128)S(1)}, u32[]{:S(2)}, u32[]{:S(2)}) async-start(f32[2,32,16,256]{3,2,1,0:T(8,128)} %fusion.7), calls=%async_computation | async-start | bytes 2097152 | tf_op jit(solution)/shard_map/all_to_all | solution.py:21
  21.6 110.3 %all-gather.3.cloned.1.call-start = ((), (), s32[]{:S(2)}) async-start(), calls=%async_computation.9 | async-start | bytes 5242880 | tf_op jit(solution)/shard_map/all_gather | solution.py:82
  78.5 23.8 %all-to-all-start.4 = ((f32[4,256,256]{2,1,0:T(8,128)}), f32[4,256,256]{2,1,0:T(8,128)S(1)}, u32[]{:S(2)}, u32[]{:S(2)}) async-start(f32[4,256,256]{2,1,0:T(8,128)} %bitcast.13), calls=%async_computation.4 | async-start | bytes 2097152 | tf_op jit(solution)/shard_map/all_to_all | solution.py:81
  82.5 415.0 %all-gather.5.cloned.1.call-start = ((), (), s32[]{:S(2)}) async-start(), calls=%async_computation.10 | async-start | bytes 5242880 | tf_op jit(solution)/shard_map/all_gather | solution.py:113
  131.9 3.4 copy-start.1
  149.8 2.0 copy-start.4
  153.6 35.4 %copy-start.3 = (f32[512,512]{1,0:T(8,128)}, f32[512,512]{1,0:T(8,128)S(1)}, u32[]{:S(2)}) copy-start(f32[512,512]{1,0:T(8,128)S(1)} %fusion.6) | copy-start | bytes 3145732
  176.0 13.1 %copy-start.9 = (f32[384,128]{1,0:T(8,128)}, f32[384,128]{1,0:T(8,128)S(1)}, u32[]{:S(2)}) copy-start(f32[384,128]{1,0:T(8,128)S(1)} %convolution_subtract_fusion.6) | copy-start | bytes 589828
  299.5 10.5 %copy-start.5 = (f32[256,128]{0,1:T(8,128)}, f32[256,128]{0,1:T(8,128)S(1)}, u32[]{:S(2)}) copy-start(f32[256,128]{0,1:T(8,128)S(1)} %fusion.78) | copy-start | bytes 393220
  300.2 9.8 %copy-start.7 = (f32[256,128]{0,1:T(8,128)}, f32[256,128]{0,1:T(8,128)S(1)}, u32[]{:S(2)}) copy-start(f32[256,128]{0,1:T(8,128)S(1)} %fusion.80) | copy-start | bytes 393220
  301.1 9.0 %copy-start.10 = (f32[256,128]{0,1:T(8,128)}, f32[256,128]{0,1:T(8,128)S(1)}, u32[]{:S(2)}) copy-start(f32[256,128]{0,1:T(8,128)S(1)} %fusion.82) | copy-start | bytes 393220
  358.9 92.3 %copy-start.6 = (f32[256,128]{0,1:T(8,128)S(1)}, f32[256,128]{0,1:T(8,128)}, u32[]{:S(2)}) copy-start(f32[256,128]{0,1:T(8,128)} %copy-done.5) | copy-start | bytes 393220
  358.9 92.3 %copy-start.8 = (f32[256,128]{0,1:T(8,128)S(1)}, f32[256,128]{0,1:T(8,128)}, u32[]{:S(2)}) copy-start(f32[256,128]{0,1:T(8,128)} %copy-done.7) | copy-start | bytes 393220
  358.9 92.3 %copy-start.11 = (f32[256,128]{0,1:T(8,128)S(1)}, f32[256,128]{0,1:T(8,128)}, u32[]{:S(2)}) copy-start(f32[256,128]{0,1:T(8,128)} %copy-done.10) | copy-start | bytes 393220
  502.7 32.0 %copy-start.2 = (f32[256,1024]{0,1:T(8,128)S(1)}, f32[256,1024]{0,1:T(8,128)}, u32[]{:S(2)}) copy-start(f32[256,1024]{0,1:T(8,128)} %maximum_maximum_fusion) | copy-start | bytes 3145732
  530.8 13.2 %all-to-all-start.7 = ((f32[32,1,1024]{2,1,0:T(1,128)}), f32[32,1,1024]{2,1,0:T(1,128)S(1)}, u32[]{:S(2)}, u32[]{:S(2)}) async-start(f32[32,1,1024]{2,1,0:T(1,128)} %reshape.234), calls=%async_computation.7 | async-start | bytes 262144 | tf_op jit(solution)/shard_map/all_to_all | solution.py:42
Sparse Core Ops, SparseCore 0:
  78.6 53.2 all-gather.2
  452.4 45.0 all-gather.4
where the time goes:
time: 566 us; the launch traced here: 562 us
  other arithmetic  251 us (44%)
  waiting for transfers between devices  103 us (18%)
  blocking collectives  83.6 us (15%)
  matrix products  53.2 us (9%)
  local copies, waits for them, and re-layouts  36.3 us (6%)
  between operations  20.1 us (4%)
  starting transfers between devices  14.9 us (3%)
    another operation x15, other arithmetic, shards(): low_two = jnp.linalg.cholesky(schur + RIDGE * identity)  79.6 us
    another operation x5, other arithmetic, right_side_solve(): lax.linalg.triangular_solve(low, values, left_side=False, lower=True, tra...  79.6 us
    another operation x14, other arithmetic, shards(): low_one = jnp.linalg.cholesky(pivot_kern[:block, :block] + RIDGE * identity)  79.5 us
    all_gather x1, waiting for transfers between devices, shards(): lax.all_gather(factor, 'cols', axis=0, tiled=True)  45.2 us
    all_to_all x2, blocking collectives, sum_by_axis(): lax.all_to_all(nearer, far, split_axis=0, concat_axis=0, tiled=True)  44.6 us
    all_to_all x3, blocking collectives, copy_for_each(): return lax.all_to_all(copies, axis, split_axis=0, concat_axis=0, tiled=True)  34.7 us
    all_gather x1, waiting for transfers between devices, shards(): pivot_full = lax.all_gather(pivot_part, 'cols', axis=1, tiled=True)  29.1 us
    all_to_all x1, waiting for transfers between devices, shards(): lax.all_to_all(points, 'cols', split_axis=0, concat_axis=1, tiled=True)  19.1 us
  transfers between devices with their start and end apart: 5, of which 5 were waited for; matrix products, arithmetic and copies ran while one was open for 0% of the time, Pallas kernels for 0%

commit v1 on v0

--- a/solution.py
+++ b/solution.py
@@ -78,7 +78,10 @@
     mine = owner == row_me
     picked = jnp.where(mine[:, None], points[inside], 0.0)
     pivot_part = sum_by_parts(picked, (("rows_0", "rows_1"), "rows_2"))
-    own_rows = lax.all_to_all(points, "cols", split_axis=0, concat_axis=1, tiled=True)
+    own_rows = jnp.concatenate(
+        lax.all_to_all(jnp.stack(jnp.split(points, lax.axis_size("cols"), axis=0)), "cols", 0, 0),
+        axis=1,
+    )
     pivot_full = lax.all_gather(pivot_part, "cols", axis=1, tiled=True)
     own_norms = jnp.sum(own_rows * own_rows, axis=1)
     full_norms = jnp.sum(pivot_full * pivot_full, axis=1)

time: 566 us -> 573 us (1.012)
  transfers between devices with their start and end apart: 5 -> 5, of which waited for: 5 -> 5; matrix products, arithmetic and copies ran while one was open for 0% -> 1% of each run, Pallas kernels for 0% -> 0%
where the time goes in v1:
time: 573 us; the launch traced here: 569 us
  other arithmetic  252 us (44%)
  waiting for transfers between devices  103 us (18%)
  blocking collectives  83.7 us (15%)
  matrix products  58.2 us (10%)
  local copies, waits for them, and re-layouts  36.6 us (6%)
  between operations  20.4 us (4%)
  starting transfers between devices  14.9 us (3%)
    another operation x5, other arithmetic, right_side_solve(): lax.linalg.triangular_solve(low, values, left_side=False, lower=True, tra...  79.7 us
    another operation x15, other arithmetic, shards(): low_two = jnp.linalg.cholesky(schur + RIDGE * identity)  79.4 us
    another operation x14, other arithmetic, shards(): low_one = jnp.linalg.cholesky(pivot_kern[:block, :block] + RIDGE * identity)  79.3 us
    all_gather x1, waiting for transfers between devices, shards(): lax.all_gather(factor, 'cols', axis=0, tiled=True)  45.2 us
    all_to_all x2, blocking collectives, sum_by_axis(): lax.all_to_all(nearer, far, split_axis=0, concat_axis=0, tiled=True)  44.6 us
    all_to_all x3, blocking collectives, copy_for_each(): return lax.all_to_all(copies, axis, split_axis=0, concat_axis=0, tiled=True)  34.9 us
    all_gather x1, waiting for transfers between devices, shards(): pivot_full = lax.all_gather(pivot_part, 'cols', axis=1, tiled=True)  27.7 us
    all_to_all x1, waiting for transfers between devices, shards(): lax.all_to_all(jnp.stack(jnp.split(points, lax.axis_size('cols'), axis=0)...  20.7 us
  transfers between devices with their start and end apart: 5, of which 5 were waited for; matrix products, arithmetic and copies ran while one was open for 1% of the time, Pallas kernels for 0%

profile of v1, /device:TPU:1, one launch (start us, length us, event | category | flops | bytes accessed | tf_op | source)
XLA Modules:
  0.0 569.0 jit_solution(16793298776348316458)
XLA Ops:
  9.0 4.7 gather_fusion
  14.8 6.8 %all-to-all-start = ((f32[2,32,16,256]{3,2,1,0:T(8,128)}), f32[2,32,16,256]{3,2,1,0:T(8,128)S(1)}, u32[]{:S(2)}, u32[]{:S(2)}) async-start(f32[2,32,16,256]{3,2,1,0:T(8,128)} %fusion.7), calls=%async_computation | async-start | bytes 2097152 | tf_op jit(solution)/shard_map/all_to_all | solution.py:21
  23.5 25.9 %all_to_all.49 = f32[32,16,256]{2,1,0:T(8,128)S(1)} all-to-all(f32[32,16,256]{2,1,0:T(8,128)S(1)} %reduce_sum.58), channel_id=1, replica_groups=mesh['rows_0'=8,'rows_1'=4,'rows_2'=2,'cols'=4] {'rows_0','rows_1'}, dimensions={0} | all-to-all | bytes 1048576 | tf_op jit(solution)/shard_map/all_to_all | solution.py:29
  49.5 20.2 %all_to_all.45 = f32[32,16,256]{2,1,0:T(8,128)S(1)} all-to-all(f32[32,16,256]{2,1,0:T(8,128)S(1)} %broadcast_in_dim.33), channel_id=1, replica_groups=mesh['rows_0'=8,'rows_1'=4,'rows_2'=2,'cols'=4] {'rows_0','rows_1'}, dimensions={0} | all-to-all | bytes 1048576 | tf_op jit(solution)/shard_map/all_to_all | solution.py:42
  69.8 7.8 %all_to_all.46 = f32[2,32,16,256]{3,2,1,0:T(8,128)S(1)} all-to-all(f32[2,32,16,256]{3,2,1,0:T(8,128)S(1)} %broadcast_in_dim.34), channel_id=1, replica_groups=mesh['rows_0'=8,'rows_1'=4,'rows_2'=2,'cols'=4] {'rows_2'}, dimensions={0} | all-to-all | bytes 2097152 | tf_op jit(solution)/shard_map/all_to_all | solution.py:42
  85.1 20.7 %all-to-all-done.4 = f32[4,256,256]{1,2,0:T(8,128)S(1)} async-done(((f32[4,256,256]{1,2,0:T(8,128)}), f32[4,256,256]{1,2,0:T(8,128)S(1)}, u32[]{:S(2)}, u32[]{:S(2)}) %all-to-all-start.4) | async-done | bytes 1048608 | tf_op jit(solution)/shard_map/all_to_all | solution.py:82
  106.0 27.7 %all-gather.3.cloned.1.call-done = f32[1024,1024]{1,0:T(8,128)} async-done(((f32[1024,256]{1,0:T(8,128)}), f32[1024,1024]{1,0:T(8,128)}) %all-gather.3.cloned.1.call-update) | async-done | bytes 4194320 | tf_op jit(solution)/shard_map/all_gather | solution.py:85
  137.2 14.6 %multiply_exponential_fusion = f32[1024,1024]{0,1:T(8,128)S(1)} fusion(f32[1024,1024]{1,0:T(8,128)S(1)} %copy-done.2, f32[1024]{0:T(1024)S(1)} %multiply_reduce_fusion), kind=kOutput, calls=%fused_computation.5 | convolution fusion | flops 12890144768 | bytes 8392704 | tf_op jit(solution)/shard_map/dot_general | solution.py:95
  155.7 11.7 %cholesky.286 = f32[128,128]{1,0:T(8,128)S(1)} custom-call(f32[128,128]{1,0:T(8,128)S(1)} %cholesky.426), custom_call_target="Cholesky" | custom-call | tf_op jit(solution)/shard_map/jit(cholesky)/cholesky | solution.py:101
  167.5 9.8 %custom-call.31 = f32[1,128,128]{1,2,0:T(8,128)S(1)} custom-call(f32[1,128,128]{2,1,0:T(8,128)S(1)} %get-tuple-element.117), custom_call_target="InvertDiagBlocksLowerTriangular" | custom-call | tf_op jit(solution)/shard_map/jit(cholesky)/cholesky | solution.py:101
  178.8 11.9 %cholesky.305 = f32[128,128]{1,0:T(8,128)S(1)} custom-call(f32[128,128]{1,0:T(8,128)S(1)} %cholesky.430), custom_call_target="Cholesky" | custom-call | tf_op jit(solution)/shard_map/jit(cholesky)/cholesky | solution.py:101
  190.9 10.4 %custom-call.32 = f32[1,128,128]{1,2,0:T(8,128)} custom-call(f32[1,128,128]{2,1,0:T(8,128)S(1)} %get-tuple-element.115), custom_call_target="InvertDiagBlocksLowerTriangular" | custom-call | tf_op jit(solution)/shard_map/jit(cholesky)/cholesky | solution.py:101
  205.1 11.7 %cholesky.326 = f32[128,128]{1,0:T(8,128)S(1)} custom-call(f32[128,128]{1,0:T(8,128)S(1)} %cholesky.435), custom_call_target="Cholesky" | custom-call | tf_op jit(solution)/shard_map/jit(cholesky)/cholesky | solution.py:101
  217.0 9.8 %custom-call.33 = f32[1,128,128]{1,2,0:T(8,128)S(1)} custom-call(f32[1,128,128]{2,1,0:T(8,128)S(1)} %get-tuple-element.113), custom_call_target="InvertDiagBlocksLowerTriangular" | custom-call | tf_op jit(solution)/shard_map/jit(cholesky)/cholesky | solution.py:101
  228.4 11.9 %cholesky.343 = f32[128,128]{1,0:T(8,128)S(1)} custom-call(f32[128,128]{1,0:T(8,128)S(1)} %convolution_subtract_fusion.16), custom_call_target="Cholesky" | custom-call | tf_op jit(solution)/shard_map/jit(cholesky)/cholesky | solution.py:101
  245.7 8.5 %while.5 = (s32[]{:T(128)}, f32[512,512]{0,1:T(8,128)S(1)}, s32[4,2]{0,1:T(2,128)S(1)}, f32[4,128,128]{2,1,0:T(8,128)S(1)}, s32[]{:T(128)}) while((s32[]{:T(128)}, f32[512,512]{0,1:T(8,128)S(1)}, s32[4,2]{0,1:T(2,128)S(1)}, f32[4,128,128]{2,1,0:T(8,128)S(1)}, s32[]{:T(128)}) %tuple.72), condition=%wide.while_cond, body=%wide.while_body.sunk | while | flops 2 | bytes 393329 | solution.py:66
  254.1 39.3 %custom-call.34 = f32[4,128,128]{1,2,0:T(8,128)S(1)} custom-call(f32[4,128,128]{2,1,0:T(8,128)S(1)} %get-tuple-element.26), custom_call_target="InvertDiagBlocksLowerTriangular" | custom-call | tf_op jit(solution)/shard_map/triangular_solve/custom-call.3 | solution.py:66
  294.8 9.7 %fusion.3 = f32[256,1024]{1,0:T(8,128)S(1)} fusion(f32[256,1024]{0,1:T(8,128)S(1)} %bitcast.144, f32[1024,1024]{1,0:T(8,128)} %all-gather.3.cloned.1.call-done, f32[1024]{0:T(1024)S(1)} %multiply_reduce_fusion, f32[256]{0:T(256)S(1)} %fusion.5), kind=kOutput, calls=%fused_computation.14 | convolution fusion | flops 3222536192 | bytes 6296576 | tf_op jit(solution)/shard_map/dot_general | solution.py:88
  319.1 11.9 %cholesky.358 = f32[128,128]{1,0:T(8,128)S(1)} custom-call(f32[128,128]{1,0:T(8,128)S(1)} %cholesky.439), custom_call_target="Cholesky" | custom-call | tf_op jit(solution)/shard_map/jit(cholesky)/cholesky | solution.py:111
  331.7 9.8 %custom-call.35 = f32[1,128,128]{1,2,0:T(8,128)S(1)} custom-call(f32[1,128,128]{2,1,0:T(8,128)S(1)} %get-tuple-element.111), custom_call_target="InvertDiagBlocksLowerTriangular" | custom-call | tf_op jit(solution)/shard_map/jit(cholesky)/cholesky | solution.py:111
  342.3 11.7 %cholesky.377 = f32[128,128]{1,0:T(8,128)S(1)} custom-call(f32[128,128]{1,0:T(8,128)S(1)} %cholesky.443), custom_call_target="Cholesky" | custom-call | tf_op jit(solution)/shard_map/jit(cholesky)/cholesky | solution.py:111
  354.7 9.8 %custom-call.36 = f32[1,128,128]{1,2,0:T(8,128)S(1)} custom-call(f32[1,128,128]{2,1,0:T(8,128)S(1)} %get-tuple-element.108), custom_call_target="InvertDiagBlocksLowerTriangular" | custom-call | tf_op jit(solution)/shard_map/jit(cholesky)/cholesky | solution.py:111
  365.3 11.9 %cholesky.398 = f32[128,128]{1,0:T(8,128)S(1)} custom-call(f32[128,128]{1,0:T(8,128)S(1)} %cholesky.448), custom_call_target="Cholesky" | custom-call | tf_op jit(solution)/shard_map/jit(cholesky)/cholesky | solution.py:111
  377.8 9.8 %custom-call.37 = f32[1,128,128]{1,2,0:T(8,128)S(1)} custom-call(f32[1,128,128]{2,1,0:T(8,128)S(1)} %get-tuple-element.105), custom_call_target="InvertDiagBlocksLowerTriangular" | custom-call | tf_op jit(solution)/shard_map/jit(cholesky)/cholesky | solution.py:111
  388.2 11.7 %cholesky.415 = f32[128,128]{1,0:T(8,128)S(1)} custom-call(f32[128,128]{1,0:T(8,128)S(1)} %convolution_subtract_fusion.15), custom_call_target="Cholesky" | custom-call | tf_op jit(solution)/shard_map/jit(cholesky)/cholesky | solution.py:111
  403.3 8.1 %while.6 = (s32[]{:T(128)}, f32[512,512]{1,0:T(8,128)S(1)}, s32[4,2]{0,1:T(2,128)S(1)}, f32[4,128,128]{2,1,0:T(8,128)S(1)}, s32[]{:T(128)}) while((s32[]{:T(128)}, f32[512,512]{1,0:T(8,128)S(1)}, s32[4,2]{0,1:T(2,128)S(1)}, f32[4,128,128]{2,1,0:T(8,128)S(1)}, s32[]{:T(128)}) %tuple.82), condition=%wide.while_cond.clone, body=%wide.while_body.clone.sunk | while | flops 2 | bytes 131189 | solution.py:66
  411.4 39.6 %custom-call.38 = f32[4,128,128]{1,2,0:T(8,128)S(1)} custom-call(f32[4,128,128]{2,1,0:T(8,128)S(1)} %get-tuple-element.27), custom_call_target="InvertDiagBlocksLowerTriangular" | custom-call | tf_op jit(solution)/shard_map/triangular_solve/custom-call.3 | solution.py:66
  458.9 45.2 %all-gather.5.cloned.1.call-done = f32[1024,1024]{0,1:T(8,128)} async-done(((f32[256,1024]{0,1:T(8,128)}), f32[1024,1024]{0,1:T(8,128)}) %all-gather.5.cloned.1.call-update) | async-done | bytes 4194320 | tf_op jit(solution)/shard_map/all_gather | solution.py:116
  504.0 5.2 fusion.99
  516.6 18.7 %all_to_all.50 = f32[32,1,1024]{2,1,0:T(1,128)S(1)} all-to-all(f32[32,1,1024]{2,1,0:T(1,128)S(1)} %reshape.237), channel_id=1, replica_groups=mesh['rows_0'=8,'rows_1'=4,'rows_2'=2,'cols'=4] {'rows_0','rows_1'}, dimensions={0} | all-to-all | bytes 262144 | tf_op jit(solution)/shard_map/all_to_all | solution.py:29
  542.5 8.0 %all-to-all-done.7 = f32[32,1,1024]{2,1,0:T(1,128)S(1)} async-done(((f32[32,1,1024]{2,1,0:T(1,128)}), f32[32,1,1024]{2,1,0:T(1,128)S(1)}, u32[]{:S(2)}, u32[]{:S(2)}) %all-to-all-start.7) | async-done | bytes 131104 | tf_op jit(solution)/shard_map/all_to_all | solution.py:42
  552.0 6.9 %all_to_all.48 = f32[2,1,32768]{2,1,0:T(1,128)S(1)} all-to-all(f32[2,1,32768]{2,1,0:T(1,128)S(1)} %reshape.241), channel_id=1, replica_groups=mesh['rows_0'=8,'rows_1'=4,'rows_2'=2,'cols'=4] {'rows_2'}, dimensions={0} | all-to-all | bytes 524288 | tf_op jit(solution)/shard_map/all_to_all | solution.py:42
  (188 shorter events, 93.6 us)
Async XLA Ops:
  7.2 496.9 %copy-start = (f32[1024,64]{0,1:T(8,128)S(1)}, f32[1024,64]{0,1:T(8,128)}, u32[]{:S(2)}) copy-start(f32[1024,64]{0,1:T(8,128)} %param.8) | copy-start | bytes 786436
  14.8 8.6 %all-to-all-start = ((f32[2,32,16,256]{3,2,1,0:T(8,128)}), f32[2,32,16,256]{3,2,1,0:T(8,128)S(1)}, u32[]{:S(2)}, u32[]{:S(2)}) async-start(f32[2,32,16,256]{3,2,1,0:T(8,128)} %fusion.7), calls=%async_computation | async-start | bytes 2097152 | tf_op jit(solution)/shard_map/all_to_all | solution.py:21
  21.6 112.1 %all-gather.3.cloned.1.call-start = ((), (), s32[]{:S(2)}) async-start(), calls=%async_computation.9 | async-start | bytes 5242880 | tf_op jit(solution)/shard_map/all_gather | solution.py:85
  49.4 29.3 %copy-start.1 = (f32[1024,256]{1,0:T(8,128)S(1)}, f32[1024,256]{1,0:T(8,128)}, u32[]{:S(2)}) copy-start(f32[1024,256]{1,0:T(8,128)} %param.6) | copy-start | bytes 3145732
  80.3 25.5 %all-to-all-start.4 = ((f32[4,256,256]{1,2,0:T(8,128)}), f32[4,256,256]{1,2,0:T(8,128)S(1)}, u32[]{:S(2)}, u32[]{:S(2)}) async-start(f32[4,256,256]{1,2,0:T(8,128)} %pad_maximum_fusion), calls=%async_computation.4 | async-start | bytes 2097152 | tf_op jit(solution)/shard_map/all_to_all | solution.py:82
  84.4 419.7 %all-gather.5.cloned.1.call-start = ((), (), s32[]{:S(2)}) async-start(), calls=%async_computation.10 | async-start | bytes 5242880 | tf_op jit(solution)/shard_map/all_gather | solution.py:116
  133.7 3.4 copy-start.2
  151.8 2.0 copy-start.5
  155.7 35.2 %copy-start.4 = (f32[512,512]{1,0:T(8,128)}, f32[512,512]{1,0:T(8,128)S(1)}, u32[]{:S(2)}) copy-start(f32[512,512]{1,0:T(8,128)S(1)} %fusion.6) | copy-start | bytes 3145732
  178.0 12.8 %copy-start.10 = (f32[384,128]{1,0:T(8,128)}, f32[384,128]{1,0:T(8,128)S(1)}, u32[]{:S(2)}) copy-start(f32[384,128]{1,0:T(8,128)S(1)} %convolution_subtract_fusion.6) | copy-start | bytes 589828
  305.5 11.0 %copy-start.6 = (f32[256,128]{0,1:T(8,128)}, f32[256,128]{0,1:T(8,128)S(1)}, u32[]{:S(2)}) copy-start(f32[256,128]{0,1:T(8,128)S(1)} %fusion.78) | copy-start | bytes 393220
  306.5 10.1 %copy-start.8 = (f32[256,128]{0,1:T(8,128)}, f32[256,128]{0,1:T(8,128)S(1)}, u32[]{:S(2)}) copy-start(f32[256,128]{0,1:T(8,128)S(1)} %fusion.80) | copy-start | bytes 393220
  307.6 9.0 %copy-start.11 = (f32[256,128]{0,1:T(8,128)}, f32[256,128]{0,1:T(8,128)S(1)}, u32[]{:S(2)}) copy-start(f32[256,128]{0,1:T(8,128)S(1)} %fusion.82) | copy-start | bytes 393220
  364.6 93.2 %copy-start.7 = (f32[256,128]{0,1:T(8,128)S(1)}, f32[256,128]{0,1:T(8,128)}, u32[]{:S(2)}) copy-start(f32[256,128]{0,1:T(8,128)} %copy-done.6) | copy-start | bytes 393220
  364.6 93.2 %copy-start.9 = (f32[256,128]{0,1:T(8,128)S(1)}, f32[256,128]{0,1:T(8,128)}, u32[]{:S(2)}) copy-start(f32[256,128]{0,1:T(8,128)} %copy-done.8) | copy-start | bytes 393220
  364.6 93.2 %copy-start.12 = (f32[256,128]{0,1:T(8,128)S(1)}, f32[256,128]{0,1:T(8,128)}, u32[]{:S(2)}) copy-start(f32[256,128]{0,1:T(8,128)} %copy-done.11) | copy-start | bytes 393220
  509.2 32.0 %copy-start.3 = (f32[256,1024]{0,1:T(8,128)S(1)}, f32[256,1024]{0,1:T(8,128)}, u32[]{:S(2)}) copy-start(f32[256,1024]{0,1:T(8,128)} %maximum_maximum_fusion) | copy-start | bytes 3145732
  537.3 13.2 %all-to-all-start.7 = ((f32[32,1,1024]{2,1,0:T(1,128)}), f32[32,1,1024]{2,1,0:T(1,128)S(1)}, u32[]{:S(2)}, u32[]{:S(2)}) async-start(f32[32,1,1024]{2,1,0:T(1,128)} %reshape.239), calls=%async_computation.7 | async-start | bytes 262144 | tf_op jit(solution)/shard_map/all_to_all | solution.py:42
Sparse Core Ops, SparseCore 0:
  78.8 54.9 all-gather.2
  459.0 45.0 all-gather.4
